TPU v7x, 32 devices: a whole 2x2x4 slice. The times are simulated.
32 devices in a mesh: seq: 32 (over z, y, x, core).
Axes of the slice: x: 2, y: 2, z: 4, core: 2. Of those that a mesh axis runs over, the one named last changes fastest.
Arguments:
- queries: bfloat16 [16384, 384], P('seq'), may hold values from -12 to 12
- keys: bfloat16 [16384, 384], P('seq'), may hold values from -6 to 6
- values: bfloat16 [16384, 384], P('seq'), may hold values from -6 to 6
- out_weight: bfloat16 [384, 768], replicated, may hold values from -0.3125 to 0.3125
Outputs:
- layer_out: bfloat16 [16384, 768], P('seq')
All inputs are finite; a program needn't handle non-finite values.
Results may differ from a plain program's by a relative error of at most 0.0054.
Values may be sent and summed in bfloat16 or wider, within the bound.
A program may use at most 128 MiB of HBM per device.

v0:
```python
import math

import jax
import jax.numpy as jnp
from jax import lax
from jax.sharding import PartitionSpec as P

HEAD_COUNT = 6
HEAD_SIZE = 64
FIRST_DILATION = 8
SECOND_DILATION = 32
THIRD_DILATION = 128


def from_partner(value, axis, bit):
    return lax.ppermute(value, axis, [(i, i ^ 1 << bit) for i in range(lax.axis_size(axis))])


def attend(query, keyval):
    rows = keyval.shape[0]
    heads = query.shape[1]
    size = query.shape[2]
    width = heads * size
    key_part = keyval[:, :width].reshape(rows, heads, size)
    value_part = keyval[:, width:].reshape(rows, heads, size)
    scores = jnp.einsum(
        "qhd,khd->hqk", query, key_part, preferred_element_type=jnp.float32
    ) / math.sqrt(size)
    top = jnp.max(scores, axis=2, keepdims=True)
    prob = jnp.exp(scores - top)
    total = jnp.sum(prob, axis=2)
    weights = prob.astype(jnp.bfloat16)
    attended = (
        jnp.einsum("hqk,khd->qhd", weights, value_part, preferred_element_type=jnp.float32)
        / total.T[:, :, None]
    )
    log_total = (top[:, :, 0] + jnp.log(total)).T
    return (attended, log_total)


def pick_rows(matrix, dilation):
    token_index = jnp.arange(HEAD_COUNT)
    shaped = matrix.reshape(matrix.shape[0] // dilation, dilation, HEAD_COUNT, HEAD_SIZE)
    return shaped[:, token_index % dilation, token_index]


def merge_pair(first_out, first_lse, second_out, second_lse):
    larger = jnp.maximum(first_lse, second_lse)
    first_w = jnp.exp(first_lse - larger)
    second_w = jnp.exp(second_lse - larger)
    summed = first_w + second_w
    merged = (first_w[..., None] * first_out + second_w[..., None] * second_out) / summed[..., None]
    return (merged, larger + jnp.log(summed))


def fold_broad_level(
    narrow_output, narrow_log_sum, broad_output, broad_log_sum, dilation_ratio, narrow_dilation
):
    token_index = jnp.arange(HEAD_COUNT)
    segment_places = token_index // narrow_dilation
    reshaped_output = narrow_output.reshape(-1, dilation_ratio, HEAD_COUNT, HEAD_SIZE)
    reshaped_log_sum = narrow_log_sum.reshape(-1, dilation_ratio, HEAD_COUNT)
    merged, merged_lse = merge_pair(
        reshaped_output[:, segment_places, token_index],
        reshaped_log_sum[:, segment_places, token_index],
        broad_output,
        broad_log_sum,
    )
    reshaped_output = reshaped_output.at[:, segment_places, token_index].set(merged)
    reshaped_log_sum = reshaped_log_sum.at[:, segment_places, token_index].set(merged_lse)
    return (
        reshaped_output.reshape(narrow_output.shape),
        reshaped_log_sum.reshape(narrow_log_sum.shape),
    )


def rows_of_level(queries, keys, values, dilation):
    width = queries.shape[1]
    picked_q = pick_rows(queries, dilation)
    count = picked_q.shape[0]
    picked_kv = jnp.concatenate(
        [
            pick_rows(keys, dilation).reshape(count, width),
            pick_rows(values, dilation).reshape(count, width),
        ],
        axis=1,
    )
    return (picked_q, picked_kv)


def widen_rows(block, bits, partner_fn):
    for bit in bits:
        block = jnp.concatenate([block, partner_fn(block, bit)], axis=0)
    return block


def short_partner(block, bit):
    return from_partner(block, "seq", bit)


def middle_partner(block, bit):
    return from_partner(block, "seq", bit)


def on_device(queries, keys, values, out_weight):
    rows_of_tokens = queries.shape[0]
    width = queries.shape[1]
    first_bits = (lax.axis_size("seq") // 16).bit_length() - 1
    second_bits = (lax.axis_size("seq") // 4).bit_length() - 1
    second_ratio = SECOND_DILATION // FIRST_DILATION
    third_ratio = THIRD_DILATION // SECOND_DILATION
    first_query, first_key_value = rows_of_level(queries, keys, values, FIRST_DILATION)
    second_query, second_key_value = rows_of_level(queries, keys, values, SECOND_DILATION)
    third_query, third_key_value = rows_of_level(queries, keys, values, THIRD_DILATION)
    near = widen_rows(first_key_value, range(first_bits), short_partner)
    middle = widen_rows(second_key_value, range(second_bits), middle_partner)
    whole = lax.all_gather(third_key_value, "seq", axis=0, tiled=True)
    block_output, block_log_sum = attend(
        queries.reshape(rows_of_tokens, HEAD_COUNT, HEAD_SIZE),
        jnp.concatenate([keys, values], axis=1),
    )
    output_third, log_sum_third = attend(third_query, whole)
    output_second, log_sum_second = attend(second_query, middle)
    output_first, log_sum_first = attend(first_query, near)
    output_second, log_sum_second = fold_broad_level(
        output_second, log_sum_second, output_third, log_sum_third, third_ratio, SECOND_DILATION
    )
    output_first, log_sum_first = fold_broad_level(
        output_first, log_sum_first, output_second, log_sum_second, second_ratio, FIRST_DILATION
    )
    token_index = jnp.arange(HEAD_COUNT)
    segment_places = token_index % FIRST_DILATION
    reshaped_output = block_output.reshape(
        rows_of_tokens // FIRST_DILATION, FIRST_DILATION, HEAD_COUNT, HEAD_SIZE
    )
    reshaped_log_sum = block_log_sum.reshape(
        rows_of_tokens // FIRST_DILATION, FIRST_DILATION, HEAD_COUNT
    )
    merged, merged_lse = merge_pair(
        reshaped_output[:, segment_places, token_index],
        reshaped_log_sum[:, segment_places, token_index],
        output_first,
        log_sum_first,
    )
    reshaped_output = reshaped_output.at[:, segment_places, token_index].set(merged)
    combined = reshaped_output.reshape(rows_of_tokens, width).astype(jnp.bfloat16)
    return jnp.dot(combined, out_weight, preferred_element_type=jnp.float32).astype(jnp.bfloat16)


def solution(mesh):
    in_specs = (P("seq", None), P("seq", None), P("seq", None), P())
    out_specs = P("seq", None)
    return jax.shard_map(
        on_device, mesh=mesh, in_specs=in_specs, out_specs=out_specs, check_vma=False
    )
```

profile of v0, /device:TPU:0, one launch (start us, length us, event | category | flops | bytes accessed | tf_op | source)
XLA Modules:
  0.0 100.5 jit_solution(3295383026716870419)
XLA Ops:
  0.0 1.7 %reshape.334 = bf16[64,8,6,64]{3,2,1,0:T(8,128)(2,1)S(1)} reshape(bf16[512,384]{1,0:T(8,128)(2,1)} %param.5) | data formatting | bytes 786432 | tf_op jit(solution)/shard_map/reshape | solution.py:43
  1.8 0.5 copy.125
  2.3 0.6 gather_fusion.2
  3.1 0.6 constant_dynamic-update-slice_fusion.1
  3.7 1.6 %reshape.336 = bf16[64,8,6,64]{3,2,1,0:T(8,128)(2,1)S(1)} reshape(bf16[512,384]{1,0:T(8,128)(2,1)} %param.6) | data formatting | bytes 786432 | tf_op jit(solution)/shard_map/reshape | solution.py:43
  5.4 0.5 copy.127
  5.9 0.6 gather_fusion.3
  6.7 0.6 constant_dynamic-update-slice_fusion
  7.3 0.5 collective-permute-start
  7.8 0.6 reshape.341
  8.4 0.6 reshape.343
  9.0 1.8 %copy.132 = bf16[16,32,6,64]{3,0,2,1:T(8,128)(2,1)} copy(bf16[16,32,6,64]{3,2,1,0:T(8,128)(2,1)S(1)} %reshape.341) | data formatting | bytes 786432 | tf_op jit(solution)/shard_map/reshape | solution.py:43
  10.8 1.7 %gather_fusion.6 = bf16[6,16,64]{2,1,0:T(8,128)(2,1)S(1)} fusion(bf16[16,32,6,64]{3,0,2,1:T(8,128)(2,1)} %copy.132, s32[6]{0:T(128)S(1)} %fusion.54), kind=kCustom, calls=%fused_computation.6 | custom fusion | bytes 24624 | tf_op jit(solution)/shard_map/gather | solution.py:44
  12.6 0.9 copy.134
  13.5 0.6 gather_fusion.7
  14.8 1.2 %copy.118 = bf16[512,384]{0,1:T(8,128)(2,1)S(1)} copy(bf16[512,384]{1,0:T(8,128)(2,1)} %param.4) | data formatting | bytes 786432 | tf_op args[0]
  16.1 0.7 copy.145
  16.8 0.6 gather_fusion.11
  17.6 0.7 copy.142
  18.2 0.6 gather_fusion.10
  18.9 43.9 %all-gather = bf16[32,4,768]{2,1,0:T(4,128)(2,1)S(1)} all-gather(bf16[1,4,768]{2,1,0:T(4,128)(2,1)S(1)} %maximum_bitcast_fusion), channel_id=1, replica_groups=mesh['seq'=32] {'seq'}, dimensions={0}, use_global_device_ids=true | all-gather | bytes 202752 | tf_op jit(solution)/shard_map/all_gather | solution.py:117
  62.9 0.6 fusion.72
  63.8 0.7 copy.140
  64.5 0.6 gather_fusion.9
  65.1 1.0 %multiply_reduce_fusion = (f32[6,512]{1,0:T(8,128)S(1)}, f32[6,512,512]{1,2,0:T(8,128)S(1)}) fusion(bf16[512,6,64]{0,2,1:T(8,128)(2,1)S(1)} %bitcast.194, bf16[512,6,64]{0,2,1:T(8,128)(2,1)S(1)} %bitcast.193), kind=kOutput, calls=%fused_computation.21 | convolution fusion | flops 204469248 | bytes 7090176 | tf_op jit(solution)/shard_map/qhd,khd->hqk/dot_general | solution.py:26
  66.1 1.0 %fusion = f32[6,512]{1,0:T(8,128)S(1)} fusion(f32[6,512,512]{1,2,0:T(8,128)S(1)} %get-tuple-element.24, f32[6,512]{1,0:T(8,128)S(1)} %get-tuple-element.23), kind=kLoop, calls=%fused_computation.22 | loop fusion | flops 4715520 | bytes 6316032 | tf_op jit(solution)/shard_map/reduce_sum | solution.py:31
  67.2 0.6 bitcast_add_fusion
  68.0 0.7 fusion.37
  68.8 2.1 %fusion.16 = f32[512,6,64]{0,2,1:T(8,128)} fusion(bf16[512,6,64]{0,2,1:T(8,128)(2,1)S(1)} %bitcast.195, f32[6,512,512]{1,2,0:T(8,128)S(1)} %get-tuple-element.24, f32[6,512]{1,0:T(8,128)S(1)} %get-tuple-element.23, f32[512,6]{0,1:T(8,128)S(1)} %bitcast.209), kind=kOutput, calls=%fused_computation.42 | convolution fusion | flops 206241792 | bytes 7495680 | tf_op jit(solution)/shard_map/hqk,khd->qhd/dot_general | solution.py:34
  70.9 0.6 pad_maximum_fusion.3
  71.5 0.6 reshape.333
  72.1 0.6 reshape.340
  72.7 1.6 %copy.160 = bf16[128,384]{0,1:T(8,128)(2,1)} copy(bf16[128,384]{1,0:T(8,128)(2,1)} %get-tuple-element.15) | data formatting | bytes 196608 | tf_op jit(solution)/shard_map/slice | solution.py:25
  74.3 0.5 copy.124
  74.8 0.6 gather_fusion.1
  75.4 0.9 copy.131
  76.4 0.6 gather_fusion.5
  76.9 0.8 reshape.332
  77.9 0.6 gather_fusion
  78.5 2.8 %copy.122 = f32[512,6,64]{2,0,1:T(8,128)} copy(f32[512,6,64]{0,2,1:T(8,128)} %fusion.16) | data formatting | bytes 1572864 | tf_op jit(solution)/shard_map/div | solution.py:34
  81.3 1.7 %copy.165 = f32[64,8,6,64]{3,0,2,1:T(8,128)S(1)} copy(f32[64,8,6,64]{3,1,0,2:T(8,128)} %bitcast.192) | data formatting | bytes 1572864 | tf_op jit(solution)/shard_map/reshape | solution.py:133
  83.0 0.6 gather_fusion.12
  83.6 0.8 pad_maximum_fusion.2
  84.4 0.9 fusion.25
  85.6 0.3 fusion.74
  85.8 0.2 fusion.23
  86.1 0.3 fusion.9
  86.7 0.6 gather_fusion.4
  87.3 0.6 gather_fusion.13
  87.9 1.5 %collective-permute-done.3 = bf16[64,768]{1,0:T(8,128)(2,1)S(1)} collective-permute-done((bf16[64,768]{1,0:T(8,128)(2,1)S(1)}, bf16[64,768]{1,0:T(8,128)(2,1)S(1)}, u32[]{:S(2)}, u32[]{:S(2)}) %collective-permute-start.3) | collective-permute-done | bytes 98336 | tf_op jit(solution)/shard_map/ppermute | solution.py:16
  89.4 0.8 pad_maximum_fusion
  91.0 0.6 gather_fusion.8
  91.7 0.8 scatter_fusion
  92.7 0.8 scatter_fusion.1
  93.8 0.2 fusion.10
  94.1 0.6 gather_fusion.14
  94.7 0.2 fusion.15
  94.9 0.8 scatter_fusion.2
  95.8 0.7 scatter_fusion.3
  96.7 0.2 fusion.21
  96.9 0.8 scatter_fusion.4
  97.9 0.5 copy.166
  98.4 0.6 convert_element_type.26
  99.0 1.5 %convolution_convert_fusion = bf16[512,768]{1,0:T(8,128)(2,1)} fusion(bf16[512,384]{1,0:T(8,128)(2,1)S(1)} %convert_element_type.26, bf16[384,768]{1,0:T(8,128)(2,1)S(1)} %copy-done), kind=kOutput, calls=%fused_computation.27 | convolution fusion | flops 302383104 | bytes 1769472 | tf_op jit(solution)/shard_map/dot_general | solution.py:147
  (82 shorter events, 4.6 us)
Async XLA Ops:
  0.0 99.0 %copy-start = (bf16[384,768]{1,0:T(8,128)(2,1)S(1)}, bf16[384,768]{1,0:T(8,128)(2,1)}, u32[]{:S(2)}) copy-start(bf16[384,768]{1,0:T(8,128)(2,1)} %param.7) | copy-start | bytes 1769476
  0.0 7.8 %copy-start.1 = (bf16[512,384]{1,0:T(8,128)(2,1)S(1)}, bf16[512,384]{1,0:T(8,128)(2,1)}, u32[]{:S(2)}) copy-start(bf16[512,384]{1,0:T(8,128)(2,1)} %param.5) | copy-start | bytes 1179652
  0.0 8.4 %copy-start.2 = (bf16[512,384]{1,0:T(8,128)(2,1)S(1)}, bf16[512,384]{1,0:T(8,128)(2,1)}, u32[]{:S(2)}) copy-start(bf16[512,384]{1,0:T(8,128)(2,1)} %param.6) | copy-start | bytes 1179652
  7.3 77.1 %collective-permute-start = (bf16[64,768]{1,0:T(8,128)(2,1)}, bf16[64,768]{1,0:T(8,128)(2,1)}, u32[]{:S(2)}, u32[]{:S(2)}) collective-permute-start(bf16[64,768]{1,0:T(8,128)(2,1)} %constant_dynamic-update-slice_fusion), channel_id=1, source_target_pairs={{0,1},{1,0},{2,3},{3,2},{4,5},{5,4},{6,7},{7,6},{8,9},{9,8},{10,11... | collective-permute-start | bytes 294920 | tf_op jit(solution)/shard_map/ppermute | solution.py:16
  14.3 56.6 %collective-permute-start.1 = (bf16[16,768]{1,0:T(8,128)(2,1)S(1)}, bf16[16,768]{1,0:T(8,128)(2,1)S(1)}, u32[]{:S(2)}, u32[]{:S(2)}) collective-permute-start(bf16[16,768]{1,0:T(8,128)(2,1)S(1)} %constant_dynamic-update-slice_fusion.2), channel_id=1, source_target_pairs={{0,1},{1,0},{2,3},{3,2},{4,5},{5,4},{6,7},{7,6},{8,9},{9,8},{10,11... | collective-permute-start | bytes 73736 | tf_op jit(solution)/shard_map/ppermute | solution.py:16
  66.1 5.4 %copy-start.3 = (bf16[512,384]{1,0:T(8,128)(2,1)S(1)}, bf16[512,384]{1,0:T(8,128)(2,1)}, u32[]{:S(2)}) copy-start(bf16[512,384]{1,0:T(8,128)(2,1)} %param.4) | copy-start | bytes 1179652
  68.0 3.5 %copy-start.5 = (f32[6,4,128]{2,1,0:T(4,128)}, f32[6,4,128]{2,1,0:T(4,128)S(1)}, u32[]{:S(2)}) copy-start(f32[6,4,128]{2,1,0:T(4,128)S(1)} %get-tuple-element.30) | copy-start | bytes 36868
  71.5 12.1 %collective-permute-start.2 = (bf16[32,768]{1,0:T(8,128)(2,1)}, bf16[32,768]{1,0:T(8,128)(2,1)}, u32[]{:S(2)}, u32[]{:S(2)}) collective-permute-start(bf16[32,768]{1,0:T(8,128)(2,1)} %pad_maximum_fusion.3), channel_id=1, source_target_pairs={{0,2},{1,3},{2,0},{3,1},{4,6},{5,7},{6,4},{7,5},{8,10},{9,11},{10,... | collective-permute-start | bytes 147464 | tf_op jit(solution)/shard_map/ppermute | solution.py:16
  76.3 15.3 %copy-start.7 = (f32[6,4]{1,0:T(8,128)S(1)}, f32[6,4]{1,0:T(8,128)}, u32[]{:S(2)}) copy-start(f32[6,4]{1,0:T(8,128)} %fusion.37) | copy-start | bytes 292
  77.8 16.9 %copy-start.4 = (bf16[128,384]{0,1:T(8,128)(2,1)S(1)}, bf16[128,384]{0,1:T(8,128)(2,1)}, u32[]{:S(2)}) copy-start(bf16[128,384]{0,1:T(8,128)(2,1)} %copy.160) | copy-start | bytes 294916
  77.8 16.9 %copy-start.6 = (f32[6,4,128]{2,1,0:T(4,128)S(1)}, f32[6,4,128]{2,1,0:T(4,128)}, u32[]{:S(2)}) copy-start(f32[6,4,128]{2,1,0:T(4,128)} %copy-done.5) | copy-start | bytes 36868
  84.4 5.0 %collective-permute-start.3 = (bf16[64,768]{1,0:T(8,128)(2,1)S(1)}, bf16[64,768]{1,0:T(8,128)(2,1)S(1)}, u32[]{:S(2)}, u32[]{:S(2)}) collective-permute-start(bf16[64,768]{1,0:T(8,128)(2,1)S(1)} %pad_maximum_fusion.2), channel_id=1, source_target_pairs={{0,4},{1,5},{2,6},{3,7},{4,0},{5,1},{6,2},{7,3},{8,12},{9,13},{10,... | collective-permute-start | bytes 294920 | tf_op jit(solution)/shard_map/ppermute | solution.py:16
where the time goes:
time: 101 us; the launch traced here: 100 us
  blocking collectives  43.9 us (43%)
  local copies, waits for them, and re-layouts  41.3 us (41%)
  other arithmetic  6.57 us (7%)
  matrix products  5.98 us (6%)
  waiting for transfers between devices  1.54 us (2%)
    all_gather x1, blocking collectives, on_device(): whole = lax.all_gather(third_key_value, 'seq', axis=0, tiled=True)  43.9 us
    reshape x18, local copies, waits for them, and re-layouts, pick_rows(): matrix.reshape(matrix.shape[0] // dilation, dilation, HEAD_COUNT, HEAD_SIZE)  13 us
    gather x15, local copies, waits for them, and re-layouts, pick_rows(): return shaped[:, token_index % dilation, token_index]  6.72 us
    concatenate x4, other arithmetic, widen_rows(): block = jnp.concatenate([block, partner_fn(block, bit)], axis=0)  3.14 us
    div x2, local copies, waits for them, and re-layouts, attend(): jnp.einsum('hqk,khd->qhd', weights, value_part, preferred_element_type=jn...  2.88 us
    dot_general x4, matrix products, attend(): jnp.einsum('hqk,khd->qhd', weights, value_part, preferred_element_type=jn...  2.81 us
    unnamed x22, local copies, waits for them, and re-layouts  2.28 us
    reduce_sum x4, other arithmetic, attend(): total = jnp.sum(prob, axis=2)  2.21 us
  transfers between devices with their start and end apart: 4, of which 1 were waited for; matrix products, arithmetic and copies ran while one was open for 36% of the time, Pallas kernels for 0%

commit v1 on v0

v1 whole, which is shorter than its diff:
```python
import functools
import math

import jax
import jax.numpy as jnp
from jax import lax
from jax.experimental import pallas as pl
from jax.experimental.pallas import tpu as pltpu
from jax.sharding import PartitionSpec as P

HEAD_COUNT = 6
HEAD_SIZE = 64
PAIRS = HEAD_COUNT // 2
FIRST_DILATION = 8
WIDTH = HEAD_COUNT * HEAD_SIZE
LANES = 2 * HEAD_SIZE
ABSENT = -1e30
SCALE = math.log2(math.e) / math.sqrt(HEAD_SIZE)
MESH = pl.DeviceIdType.MESH
QUERY_CHUNK = 256


def iota(shape, axis):
    return lax.broadcasted_iota(jnp.int32, shape, axis)


def one_hot_rows(pair, tokens):
    row = iota((LANES, 1), 0)
    half = row >> 6
    slot = row & 63
    turned = (slot - 4 * pair) & 15
    rest = turned - 4
    third = rest * 43 >> 7
    second_place = jnp.where(turned < 4, 16 * turned, 16 * third + 4 * (rest - 3 * third + 1))
    other = slot - 16
    third = other * 43 >> 7
    first_place = 4 * third + (other - 3 * third) + 1
    place = jnp.where(slot < 16, second_place, first_place)
    token = FIRST_DILATION * place + 2 * pair + half
    return jnp.where(iota((LANES, tokens), 1) == token, 1.0, 0.0).astype(jnp.bfloat16)


def dot(a, b, dims=((1,), (0,))):
    return lax.dot_general(a, b, (dims, ((), ())), preferred_element_type=jnp.float32)


def partial_softmax(scores, value, value_dim):
    top = jnp.max(scores, axis=0, keepdims=True)
    prob = jnp.exp2((scores - top) * SCALE)
    total = jnp.sum(prob, axis=0, keepdims=True)
    return top, total, dot(value, prob.astype(jnp.bfloat16), ((value_dim,), (0,)))


def join(parts):
    top = functools.reduce(jnp.maximum, [p[0] for p in parts])
    weights = [jnp.exp2((p[0] - top) * SCALE) for p in parts]
    total = sum(w * p[1] for w, p in zip(weights, parts))
    return sum(w * p[2] for w, p in zip(weights, parts)) * (1.0 / total)


def kernel(
    chips, q_hbm, k_hbm, v_hbm, w_hbm, out_hbm,
    q_ref, k_ref, v_ref, w_ref, out_ref, comb, spread, vt, qbd, near, middle, whole,
    in_sem, out_sem, send_sem, recv_sem, mate_send, mate_recv,
):
    tokens = q_ref.shape[0]
    me = lax.axis_index("seq")
    chip = lax.div(me, 2)
    core = lax.rem(me, 2)
    mate = chip * 2 + 1 - core
    bufs = (near, middle, whole)

    loads = []
    for n, (src, dst) in enumerate(((k_hbm, k_ref), (v_hbm, v_ref), (q_hbm, q_ref), (w_hbm, w_ref))):
        loads.append(pltpu.make_async_copy(src, dst, in_sem.at[n]))
        loads[-1].start()

    barrier = pltpu.get_barrier_semaphore()
    pl.semaphore_signal(barrier, inc=1, device_id=(mate,), device_id_type=MESH)

    def over(count, body):
        if count <= 16:
            for d in range(1, count):
                body(d)
        else:
            lax.fori_loop(1, count, lambda d, _: (body(d), 0)[1], 0)

    def peer(count, d):
        place = lax.rem(chip, count)
        return (chip - place + lax.rem(place + d, count)) * 2 + core

    total_chips = chips[2]

    def greet(d):
        pl.semaphore_signal(
            barrier, inc=1, device_id=(peer(total_chips, d),), device_id_type=MESH
        )

    over(total_chips, greet)

    block_diagonal = (iota((LANES, LANES), 0) >> 6) == (iota((LANES, LANES), 1) >> 6)
    for t in range(PAIRS):
        spread[t] = one_hot_rows(t, tokens)

    places = [lax.rem(chip, c) for c in chips]
    slot_pair = iota((16, LANES), 0) >> 2
    for n, src in enumerate((k_ref, v_ref)):
        loads[n].wait()
        packed = jnp.zeros((16, LANES), jnp.float32)
        for t in range(PAIRS):
            picked = dot(spread[t], src[:, t * LANES:(t + 1) * LANES])
            picked = jnp.where(block_diagonal, picked, 0.0)
            rows = picked[:HEAD_SIZE] + picked[HEAD_SIZE:]
            packed = jnp.where(slot_pair == t, rows[:16], packed)
            rows = rows.astype(jnp.bfloat16)
            first = n * WIDTH + t * LANES
            near[core, places[0], :, first:first + LANES] = rows
            middle[core, places[1], :, first:first + LANES] = rows[:16]
        whole[core, places[2], :, n * LANES:(n + 1) * LANES] = packed.astype(jnp.bfloat16)

    pl.semaphore_wait(barrier, total_chips)

    for level in (2, 1, 0):
        own = bufs[level].at[core, places[level]]

        def send(d, level=level, own=own):
            pltpu.make_async_remote_copy(
                src_ref=own,
                dst_ref=own,
                send_sem=send_sem.at[level],
                recv_sem=recv_sem.at[level],
                device_id=(peer(chips[level], d),),
                device_id_type=MESH,
            ).start()

        over(chips[level], send)

    def to_mate(level):
        part = bufs[level].at[core]
        return pltpu.make_async_remote_copy(
            src_ref=part,
            dst_ref=part,
            send_sem=mate_send.at[level],
            recv_sem=mate_recv.at[level],
            device_id=(mate,),
            device_id_type=MESH,
        )

    def others(level, sem):
        part = bufs[level].at[core, pl.ds(0, chips[level] - 1)]
        return pltpu.make_async_copy(part, part, sem.at[level])

    def forward(level):
        if chips[level] > 1:
            others(level, recv_sem).wait()
        to_mate(level).start()

    if chips[0] == 1:
        forward(0)

    vt[...] = v_ref[...].T
    loads[2].wait()
    for t in range(PAIRS):
        picked = dot(spread[t], q_ref[:, t * LANES:(t + 1) * LANES])
        qbd[t] = jnp.where(block_diagonal, picked, 0.0).astype(jnp.bfloat16)

    lane_half = iota((QUERY_CHUNK, LANES), 1) >> 6

    def local_heads(heads):
        for h in heads:
            t, e = divmod(h, 2)
            key = k_ref[:, t * LANES:(t + 1) * LANES]
            value = vt[h * HEAD_SIZE:(h + 1) * HEAD_SIZE]
            for first in range(0, tokens, QUERY_CHUNK):
                query = q_ref[first:first + QUERY_CHUNK, t * LANES:(t + 1) * LANES]
                query = jnp.where(lane_half == e, query, jnp.zeros_like(query))
                _, total, out = partial_softmax(dot(key, query, ((1,), (1,))), value, 1)
                comb[h * HEAD_SIZE:(h + 1) * HEAD_SIZE, first:first + QUERY_CHUNK] = (
                    out * (1.0 / total)
                ).astype(jnp.bfloat16)

    local_heads(range(0, 3))
    for level in (1, 2) if chips[0] == 1 else (0, 1, 2):
        forward(level)
    local_heads(range(3, HEAD_COUNT))

    parts = []
    for t in range(PAIRS):
        columns = slice(t * LANES, (t + 1) * LANES)
        scores = dot(k_ref[:, columns], qbd[t], ((1,), (1,)))
        parts.append([partial_softmax(scores, vt[columns], 1)])

    for level in range(3):
        to_mate(level).wait()

    def rows_of(buf, first):
        block = buf[:, :, :, first:first + LANES]
        return block.reshape(-1, LANES)

    lane_slot = iota((1, LANES), 1) & 63
    slot_rows = (iota((LANES, LANES), 0) & 63) >> 2
    query = jnp.zeros((LANES, LANES), jnp.float32)
    for t in range(PAIRS):
        query = jnp.where(slot_rows == t, qbd[t].astype(jnp.float32), query)
    scores = dot(rows_of(whole, 0), query.astype(jnp.bfloat16), ((1,), (1,)))
    row_pair = (iota(scores.shape, 0) & 15) >> 2
    scores = jnp.where(row_pair == (lane_slot >> 2), scores, ABSENT)
    top3, total3, out3 = partial_softmax(scores, rows_of(whole, LANES), 0)

    for t in range(PAIRS):
        columns = slice(t * LANES, (t + 1) * LANES)
        scores = dot(rows_of(near, t * LANES), qbd[t], ((1,), (1,)))
        parts[t].append(partial_softmax(scores, rows_of(near, WIDTH + t * LANES), 0))
        scores = dot(rows_of(middle, t * LANES), qbd[t], ((1,), (1,)))
        top, total, out = partial_softmax(scores, rows_of(middle, WIDTH + t * LANES), 0)
        parts[t].append((jnp.where(lane_slot < 16, top, ABSENT), total, out))
        parts[t].append((jnp.where((lane_slot >> 2) == t, top3, ABSENT), total3, out3))
        merged = jnp.where(block_diagonal, join(parts[t]), 0.0).astype(jnp.bfloat16)
        placed = dot(merged, spread[t])
        head = 2 * t + (iota(placed.shape, 0) >> 6)
        chosen = (iota(placed.shape, 1) & (FIRST_DILATION - 1)) == head
        comb[columns] = jnp.where(
            chosen, placed, comb[columns].astype(jnp.float32)
        ).astype(jnp.bfloat16)

    loads[3].wait()
    stores = []
    for n, first in enumerate(range(0, tokens, QUERY_CHUNK)):
        rows = slice(first, first + QUERY_CHUNK)
        out_ref[rows] = dot(comb[:, rows].T, w_ref[...]).astype(jnp.bfloat16)
        stores.append(pltpu.make_async_copy(out_ref.at[rows], out_hbm.at[rows], out_sem.at[n]))
        stores[-1].start()

    for level in range(3):
        if chips[level] > 1:
            others(level, send_sem).wait()
    for store in stores:
        store.wait()


def on_device(queries, keys, values, out_weight):
    devices = lax.axis_size("seq")
    tokens = queries.shape[0]
    columns = out_weight.shape[1]
    chips = (devices // 32, devices // 8, devices // 2)
    bf16 = jnp.bfloat16
    slots = tokens // FIRST_DILATION
    return pl.pallas_call(
        functools.partial(kernel, chips),
        out_shape=jax.ShapeDtypeStruct((tokens, columns), bf16),
        in_specs=[pl.BlockSpec(memory_space=pl.ANY)] * 4,
        out_specs=pl.BlockSpec(memory_space=pl.ANY),
        scratch_shapes=[
            pltpu.VMEM(queries.shape, bf16),
            pltpu.VMEM(keys.shape, bf16),
            pltpu.VMEM(values.shape, bf16),
            pltpu.VMEM(out_weight.shape, bf16),
            pltpu.VMEM((tokens, columns), bf16),
            pltpu.VMEM((WIDTH, tokens), bf16),
            pltpu.VMEM((PAIRS, LANES, tokens), bf16),
            pltpu.VMEM((WIDTH, tokens), bf16),
            pltpu.VMEM((PAIRS, LANES, LANES), bf16),
            pltpu.VMEM((2, chips[0], slots, 2 * WIDTH), bf16),
            pltpu.VMEM((2, chips[1], slots // 4, 2 * WIDTH), bf16),
            pltpu.VMEM((2, chips[2], 16, 2 * LANES), bf16),
            pltpu.SemaphoreType.DMA((4,)),
            pltpu.SemaphoreType.DMA((tokens // QUERY_CHUNK,)),
            pltpu.SemaphoreType.DMA((3,)),
            pltpu.SemaphoreType.DMA((3,)),
            pltpu.SemaphoreType.DMA((3,)),
            pltpu.SemaphoreType.DMA((3,)),
        ],
        compiler_params=pltpu.CompilerParams(
            collective_id=0, has_side_effects=True, vmem_limit_bytes=56 * 1024 * 1024
        ),
        cost_estimate=pl.CostEstimate(
            flops=1_000_000_000, bytes_accessed=3_000_000, transcendentals=2_000_000
        ),
    )(queries, keys, values, out_weight)


def solution(mesh):
    in_specs = (P("seq", None), P("seq", None), P("seq", None), P())
    return jax.shard_map(
        on_device, mesh=mesh, in_specs=in_specs, out_specs=P("seq", None), check_vma=False
    )
```

time: 101 us -> 18.7 us (0.19)
  blocking collectives: 43.9 us -> 0 us
  local copies, waits for them, and re-layouts: 41.3 us -> 2.06 us
  Pallas kernels: 0 us -> 16.4 us
  other arithmetic: 6.57 us -> 0 us
  matrix products: 5.98 us -> 0 us
  waiting for transfers between devices: 1.54 us -> 0 us
    all_gather x1 -> x0, blocking collectives: 43.9 us -> none  [on_device(): whole = lax.all_gather(third_key_value, 'seq', axis=0, tiled=True)]
    reshape x34 -> x0, local copies, waits for them, and re-layouts: 16.9 us -> none  [the longest x18 13 us: pick_rows(): matrix.reshape(matrix.shape[0] // dilation, dilation, HEAD_COUNT, HEAD_SIZE)]
    pallas_call x0 -> x1, Pallas kernels: none -> 16.4 us  [on_device(): pl.pallas_call(functools.partial(kernel, chips), out_shape=jax.ShapeDtype...]
    gather x21 -> x0, local copies, waits for them, and re-layouts: 10.3 us -> none  [the longest x15 6.72 us: pick_rows(): return shaped[:, token_index % dilation, token_index]]
    dot_general x9 -> x0, matrix products: 5.98 us -> none  [the longest x4 2.81 us: attend(): jnp.einsum('hqk,khd->qhd', weights, value_part, preferred_element_type=jn...]
    scatter x9 -> x0, local copies, waits for them, and re-layouts: 4.22 us -> none  [the longest x4 1.81 us: fold_broad_level(): reshaped_log_sum.at[:, segment_places, token_index].set(merged_lse)]
    concatenate x12 -> x0, other arithmetic: 3.22 us -> none  [the longest x4 3.14 us: widen_rows(): block = jnp.concatenate([block, partner_fn(block, bit)], axis=0)]
    slice x8 -> x0, local copies, waits for them, and re-layouts: 2.91 us -> none  [the longest x3 1.88 us: attend(): value_part = keyval[:, width:].reshape(rows, heads, size)]
  transfers between devices with their start and end apart: 4 -> 0, of which waited for: 1 -> 0; matrix products, arithmetic and copies ran while one was open for 36% -> 0% of each run, Pallas kernels for 0% -> 0%
where the time goes in v1:
time: 18.7 us; the launch traced here: 18.5 us
  Pallas kernels  16.4 us (88%)
  local copies, waits for them, and re-layouts  2.06 us (11%)
    pallas_call x1, Pallas kernels, on_device(): pl.pallas_call(functools.partial(kernel, chips), out_shape=jax.ShapeDtype...  16.4 us
    unnamed x1, local copies, waits for them, and re-layouts  2.06 us

profile of v1, /device:TPU:0, one launch (start us, length us, event | category | flops | bytes accessed | tf_op | source)
XLA Modules:
  0.0 18.5 jit_solution(9990527731301640337)
XLA Ops:
  0.0 16.4 %shard_map.46 = bf16[512,768]{1,0:T(8,128)(2,1)} custom-call(bf16[512,384]{1,0:T(8,128)(2,1)} %q_hbm.1, bf16[512,384]{1,0:T(8,128)(2,1)} %k_hbm.1, bf16[512,384]{1,0:T(8,128)(2,1)} %v_hbm.1, bf16[384,768]{1,0:T(8,128)(2,1)} %w_hbm.1), custom_call_target="tpu_custom_call" | custom-call | flops 1000000000 | bytes 3000000 | tf_op jit(solution)/shard_map/pallas_call | solution.py:248
  16.4 2.1 %copy.6 = bf16[512,768]{1,0:T(8,128)(2,1)} copy(bf16[512,768]{1,0:T(8,128)(2,1)} %shard_map.46) | data formatting | bytes 1572864

commit v2 on v1

--- a/solution.py
+++ b/solution.py
@@ -17,6 +17,7 @@
 ABSENT = -1e30
 SCALE = math.log2(math.e) / math.sqrt(HEAD_SIZE)
 MESH = pl.DeviceIdType.MESH
+VMEM_LIMIT = int(53.35 * 1024 * 1024)
 QUERY_CHUNK = 256
 
 
@@ -59,8 +60,8 @@
 
 
 def kernel(
-    chips, q_hbm, k_hbm, v_hbm, w_hbm, out_hbm,
-    q_ref, k_ref, v_ref, w_ref, out_ref, comb, spread, vt, qbd, near, middle, whole,
+    chips, q_hbm, k_hbm, v_hbm, out_hbm,
+    q_ref, k_ref, v_ref, comb, spread, vt, qt, qbd, near, middle, whole,
     in_sem, out_sem, send_sem, recv_sem, mate_send, mate_recv,
 ):
     tokens = q_ref.shape[0]
@@ -71,7 +72,7 @@
     bufs = (near, middle, whole)
 
     loads = []
-    for n, (src, dst) in enumerate(((k_hbm, k_ref), (v_hbm, v_ref), (q_hbm, q_ref), (w_hbm, w_ref))):
+    for n, (src, dst) in enumerate(((k_hbm, k_ref), (v_hbm, v_ref), (q_hbm, q_ref))):
         loads.append(pltpu.make_async_copy(src, dst, in_sem.at[n]))
         loads[-1].start()
 
@@ -164,20 +165,28 @@
         picked = dot(spread[t], q_ref[:, t * LANES:(t + 1) * LANES])
         qbd[t] = jnp.where(block_diagonal, picked, 0.0).astype(jnp.bfloat16)
 
-    lane_half = iota((QUERY_CHUNK, LANES), 1) >> 6
+    for t in range(PAIRS):
+        turned = q_ref[:, t * LANES:(t + 1) * LANES].T
+        for e in range(2):
+            mine = (iota(turned.shape, 0) >> 6) == e
+            qt[2 * t + e] = jnp.where(mine, turned, jnp.zeros_like(turned))
 
     def local_heads(heads):
-        for h in heads:
-            t, e = divmod(h, 2)
-            key = k_ref[:, t * LANES:(t + 1) * LANES]
-            value = vt[h * HEAD_SIZE:(h + 1) * HEAD_SIZE]
-            for first in range(0, tokens, QUERY_CHUNK):
-                query = q_ref[first:first + QUERY_CHUNK, t * LANES:(t + 1) * LANES]
-                query = jnp.where(lane_half == e, query, jnp.zeros_like(query))
-                _, total, out = partial_softmax(dot(key, query, ((1,), (1,))), value, 1)
-                comb[h * HEAD_SIZE:(h + 1) * HEAD_SIZE, first:first + QUERY_CHUNK] = (
-                    out * (1.0 / total)
-                ).astype(jnp.bfloat16)
+        chunks = [(h, first) for h in heads for first in range(0, tokens, QUERY_CHUNK)]
+
+        def scores_of(chunk):
+            h, first = chunk
+            t = h // 2
+            return dot(k_ref[:, t * LANES:(t + 1) * LANES], qt[h, :, first:first + QUERY_CHUNK])
+
+        ahead = scores_of(chunks[0])
+        for n, (h, first) in enumerate(chunks):
+            scores = ahead
+            if n + 1 < len(chunks):
+                ahead = scores_of(chunks[n + 1])
+            rows = slice(h * HEAD_SIZE, (h + 1) * HEAD_SIZE)
+            _, total, out = partial_softmax(scores, vt[rows], 1)
+            comb[rows, first:first + QUERY_CHUNK] = (out * (1.0 / total)).astype(jnp.bfloat16)
 
     local_heads(range(0, 3))
     for level in (1, 2) if chips[0] == 1 else (0, 1, 2):
@@ -190,30 +199,39 @@
         scores = dot(k_ref[:, columns], qbd[t], ((1,), (1,)))
         parts.append([partial_softmax(scores, vt[columns], 1)])
 
-    for level in range(3):
-        to_mate(level).wait()
-
     def rows_of(buf, first):
         block = buf[:, :, :, first:first + LANES]
         return block.reshape(-1, LANES)
 
+    def shared_level(buf, t):
+        scores = dot(rows_of(buf, t * LANES), qbd[t], ((1,), (1,)))
+        return partial_softmax(scores, rows_of(buf, WIDTH + t * LANES), 0)
+
     lane_slot = iota((1, LANES), 1) & 63
     slot_rows = (iota((LANES, LANES), 0) & 63) >> 2
     query = jnp.zeros((LANES, LANES), jnp.float32)
     for t in range(PAIRS):
         query = jnp.where(slot_rows == t, qbd[t].astype(jnp.float32), query)
-    scores = dot(rows_of(whole, 0), query.astype(jnp.bfloat16), ((1,), (1,)))
+    query = query.astype(jnp.bfloat16)
+
+    to_mate(0).wait()
+    for t in range(PAIRS):
+        parts[t].append(shared_level(near, t))
+
+    to_mate(1).wait()
+    for t in range(PAIRS):
+        top, total, out = shared_level(middle, t)
+        parts[t].append((jnp.where(lane_slot < 16, top, ABSENT), total, out))
+
+    to_mate(2).wait()
+    scores = dot(rows_of(whole, 0), query, ((1,), (1,)))
     row_pair = (iota(scores.shape, 0) & 15) >> 2
     scores = jnp.where(row_pair == (lane_slot >> 2), scores, ABSENT)
     top3, total3, out3 = partial_softmax(scores, rows_of(whole, LANES), 0)
 
+    stores = []
     for t in range(PAIRS):
         columns = slice(t * LANES, (t + 1) * LANES)
-        scores = dot(rows_of(near, t * LANES), qbd[t], ((1,), (1,)))
-        parts[t].append(partial_softmax(scores, rows_of(near, WIDTH + t * LANES), 0))
-        scores = dot(rows_of(middle, t * LANES), qbd[t], ((1,), (1,)))
-        top, total, out = partial_softmax(scores, rows_of(middle, WIDTH + t * LANES), 0)
-        parts[t].append((jnp.where(lane_slot < 16, top, ABSENT), total, out))
         parts[t].append((jnp.where((lane_slot >> 2) == t, top3, ABSENT), total3, out3))
         merged = jnp.where(block_diagonal, join(parts[t]), 0.0).astype(jnp.bfloat16)
         placed = dot(merged, spread[t])
@@ -222,13 +240,7 @@
         comb[columns] = jnp.where(
             chosen, placed, comb[columns].astype(jnp.float32)
         ).astype(jnp.bfloat16)
-
-    loads[3].wait()
-    stores = []
-    for n, first in enumerate(range(0, tokens, QUERY_CHUNK)):
-        rows = slice(first, first + QUERY_CHUNK)
-        out_ref[rows] = dot(comb[:, rows].T, w_ref[...]).astype(jnp.bfloat16)
-        stores.append(pltpu.make_async_copy(out_ref.at[rows], out_hbm.at[rows], out_sem.at[n]))
+        stores.append(pltpu.make_async_copy(comb.at[columns], out_hbm.at[columns], out_sem.at[t]))
         stores[-1].start()
 
     for level in range(3):
@@ -241,42 +253,41 @@
 def on_device(queries, keys, values, out_weight):
     devices = lax.axis_size("seq")
     tokens = queries.shape[0]
-    columns = out_weight.shape[1]
     chips = (devices // 32, devices // 8, devices // 2)
     bf16 = jnp.bfloat16
     slots = tokens // FIRST_DILATION
-    return pl.pallas_call(
+    combined = pl.pallas_call(
         functools.partial(kernel, chips),
-        out_shape=jax.ShapeDtypeStruct((tokens, columns), bf16),
-        in_specs=[pl.BlockSpec(memory_space=pl.ANY)] * 4,
+        out_shape=jax.ShapeDtypeStruct((WIDTH, tokens), bf16),
+        in_specs=[pl.BlockSpec(memory_space=pl.ANY)] * 3,
         out_specs=pl.BlockSpec(memory_space=pl.ANY),
         scratch_shapes=[
             pltpu.VMEM(queries.shape, bf16),
             pltpu.VMEM(keys.shape, bf16),
             pltpu.VMEM(values.shape, bf16),
-            pltpu.VMEM(out_weight.shape, bf16),
-            pltpu.VMEM((tokens, columns), bf16),
             pltpu.VMEM((WIDTH, tokens), bf16),
             pltpu.VMEM((PAIRS, LANES, tokens), bf16),
             pltpu.VMEM((WIDTH, tokens), bf16),
+            pltpu.VMEM((HEAD_COUNT, LANES, tokens), bf16),
             pltpu.VMEM((PAIRS, LANES, LANES), bf16),
             pltpu.VMEM((2, chips[0], slots, 2 * WIDTH), bf16),
             pltpu.VMEM((2, chips[1], slots // 4, 2 * WIDTH), bf16),
             pltpu.VMEM((2, chips[2], 16, 2 * LANES), bf16),
-            pltpu.SemaphoreType.DMA((4,)),
-            pltpu.SemaphoreType.DMA((tokens // QUERY_CHUNK,)),
+            pltpu.SemaphoreType.DMA((3,)),
+            pltpu.SemaphoreType.DMA((PAIRS,)),
             pltpu.SemaphoreType.DMA((3,)),
             pltpu.SemaphoreType.DMA((3,)),
             pltpu.SemaphoreType.DMA((3,)),
             pltpu.SemaphoreType.DMA((3,)),
         ],
         compiler_params=pltpu.CompilerParams(
-            collective_id=0, has_side_effects=True, vmem_limit_bytes=56 * 1024 * 1024
+            collective_id=0, has_side_effects=True, vmem_limit_bytes=VMEM_LIMIT
         ),
         cost_estimate=pl.CostEstimate(
             flops=1_000_000_000, bytes_accessed=3_000_000, transcendentals=2_000_000
         ),
-    )(queries, keys, values, out_weight)
+    )(queries, keys, values)
+    return dot(combined, out_weight, ((0,), (0,))).astype(bf16)
 
 
 def solution(mesh):

time: 18.7 us -> 16.8 us (0.90)
  local copies, waits for them, and re-layouts: 2.06 us -> 0.01 us
  matrix products: 0 us -> 1.48 us
  Pallas kernels: 16.4 us -> 15.2 us
    unnamed x1 -> x2, local copies, waits for them, and re-layouts: 2.06 us -> 0.01 us
    dot_general x0 -> x1, matrix products: none -> 1.48 us  [dot(): lax.dot_general(a, b, (dims, ((), ())), preferred_element_type=jnp.float32)]
    pallas_call x1, Pallas kernels: 16.4 us -> 15.2 us  [on_device(): pl.pallas_call(functools.partial(kernel, chips), out_shape=jax.ShapeDtype...]
where the time goes in v2:
time: 16.8 us; the launch traced here: 16.7 us
  Pallas kernels  15.2 us (90%)
  matrix products  1.48 us (9%)
    pallas_call x1, Pallas kernels, on_device(): pl.pallas_call(functools.partial(kernel, chips), out_shape=jax.ShapeDtype...  15.2 us
    dot_general x1, matrix products, dot(): lax.dot_general(a, b, (dims, ((), ())), preferred_element_type=jnp.float32)  1.48 us

profile of v2, /device:TPU:0, one launch (start us, length us, event | category | flops | bytes accessed | tf_op | source)
XLA Modules:
  0.0 16.7 jit_solution(9065371120028291547)
XLA Ops:
  0.0 0.0 copy-start
  0.0 15.2 %shard_map.46 = bf16[384,512]{1,0:T(8,128)(2,1)S(1)} custom-call(bf16[512,384]{1,0:T(8,128)(2,1)} %q_hbm.1, bf16[512,384]{1,0:T(8,128)(2,1)} %k_hbm.1, bf16[512,384]{1,0:T(8,128)(2,1)} %v_hbm.1), custom_call_target="tpu_custom_call" | custom-call | flops 1000000000 | bytes 3000000 | tf_op jit(solution)/shard_map/pallas_call | solution.py:259
  15.2 0.0 copy-done
  15.2 1.5 %convolution_convert_fusion = bf16[512,768]{1,0:T(8,128)(2,1)} fusion(bf16[384,512]{1,0:T(8,128)(2,1)S(1)} %shard_map.46, bf16[384,768]{1,0:T(8,128)(2,1)S(1)} %copy-done), kind=kOutput, calls=%fused_computation | convolution fusion | flops 302383104 | bytes 1769472 | tf_op jit(solution)/shard_map/dot_general | solution.py:45
Async XLA Ops:
  0.0 15.2 %copy-start = (bf16[384,768]{1,0:T(8,128)(2,1)S(1)}, bf16[384,768]{1,0:T(8,128)(2,1)}, u32[]{:S(2)}) copy-start(bf16[384,768]{1,0:T(8,128)(2,1)} %param.7) | copy-start | bytes 1769476

commit v3 on v2

--- a/solution.py
+++ b/solution.py
@@ -17,6 +17,8 @@
 ABSENT = -1e30
 SCALE = math.log2(math.e) / math.sqrt(HEAD_SIZE)
 MESH = pl.DeviceIdType.MESH
+HALF_FIRST = 4
+ALL_FIRST = 1
 VMEM_LIMIT = int(53.35 * 1024 * 1024)
 QUERY_CHUNK = 256
 
@@ -52,16 +54,16 @@
     return top, total, dot(value, prob.astype(jnp.bfloat16), ((value_dim,), (0,)))
 
 
-def join(parts):
-    top = functools.reduce(jnp.maximum, [p[0] for p in parts])
-    weights = [jnp.exp2((p[0] - top) * SCALE) for p in parts]
-    total = sum(w * p[1] for w, p in zip(weights, parts))
-    return sum(w * p[2] for w, p in zip(weights, parts)) * (1.0 / total)
+def join(a, b):
+    top = jnp.maximum(a[0], b[0])
+    a_weight = jnp.exp2((a[0] - top) * SCALE)
+    b_weight = jnp.exp2((b[0] - top) * SCALE)
+    return top, a_weight * a[1] + b_weight * b[1], a_weight * a[2] + b_weight * b[2]
 
 
 def kernel(
     chips, q_hbm, k_hbm, v_hbm, out_hbm,
-    q_ref, k_ref, v_ref, comb, spread, vt, qt, qbd, near, middle, whole,
+    q_ref, k_ref, v_ref, comb, spread, vt, qt, qbd, tops, totals, sums, near, middle, whole,
     in_sem, out_sem, send_sem, recv_sem, mate_send, mate_recv,
 ):
     tokens = q_ref.shape[0]
@@ -88,7 +90,7 @@
 
     def peer(count, d):
         place = lax.rem(chip, count)
-        return (chip - place + lax.rem(place + d, count)) * 2 + core
+        return (chip - place + d - jnp.where(d <= place, 1, 0)) * 2 + core
 
     total_chips = chips[2]
 
@@ -119,6 +121,57 @@
             middle[core, places[1], :, first:first + LANES] = rows[:16]
         whole[core, places[2], :, n * LANES:(n + 1) * LANES] = packed.astype(jnp.bfloat16)
 
+    def prepare():
+        vt[...] = v_ref[...].T
+        loads[2].wait()
+        for t in range(PAIRS):
+            picked = dot(spread[t], q_ref[:, t * LANES:(t + 1) * LANES])
+            qbd[t] = jnp.where(block_diagonal, picked, 0.0).astype(jnp.bfloat16)
+
+        for t in range(PAIRS):
+            turned = q_ref[:, t * LANES:(t + 1) * LANES].T
+            for e in range(2):
+                mine = (iota(turned.shape, 0) >> 6) == e
+                qt[2 * t + e] = jnp.where(mine, turned, jnp.zeros_like(turned))
+
+    def local_heads(heads):
+        chunks = [(h, first) for h in heads for first in range(0, tokens, QUERY_CHUNK)]
+
+        def scores_of(chunk):
+            h, first = chunk
+            t = h // 2
+            return dot(k_ref[:, t * LANES:(t + 1) * LANES], qt[h, :, first:first + QUERY_CHUNK])
+
+        ahead = scores_of(chunks[0])
+        for n, (h, first) in enumerate(chunks):
+            scores = ahead
+            if n + 1 < len(chunks):
+                ahead = scores_of(chunks[n + 1])
+            rows = slice(h * HEAD_SIZE, (h + 1) * HEAD_SIZE)
+            _, total, out = partial_softmax(scores, vt[rows], 1)
+            comb[rows, first:first + QUERY_CHUNK] = (out * (1.0 / total)).astype(jnp.bfloat16)
+
+    def first_half():
+        prepare()
+        local_heads(range(0, 3))
+
+    def second_half():
+        local_heads(range(3, HEAD_COUNT))
+        for t in range(PAIRS):
+            columns = slice(t * LANES, (t + 1) * LANES)
+            scores = dot(k_ref[:, columns], qbd[t], ((1,), (1,)))
+            top, total, out = partial_softmax(scores, vt[columns], 1)
+            tops[t], totals[t], sums[t] = top, total, out
+
+    def before(bound, work):
+        pl.when(chip < bound)(work)
+
+    def after(bound, work):
+        pl.when(chip >= bound)(work)
+
+    before(HALF_FIRST, first_half)
+    before(ALL_FIRST, second_half)
+
     pl.semaphore_wait(barrier, total_chips)
 
     for level in (2, 1, 0):
@@ -159,45 +212,12 @@
     if chips[0] == 1:
         forward(0)
 
-    vt[...] = v_ref[...].T
-    loads[2].wait()
-    for t in range(PAIRS):
-        picked = dot(spread[t], q_ref[:, t * LANES:(t + 1) * LANES])
-        qbd[t] = jnp.where(block_diagonal, picked, 0.0).astype(jnp.bfloat16)
-
-    for t in range(PAIRS):
-        turned = q_ref[:, t * LANES:(t + 1) * LANES].T
-        for e in range(2):
-            mine = (iota(turned.shape, 0) >> 6) == e
-            qt[2 * t + e] = jnp.where(mine, turned, jnp.zeros_like(turned))
-
-    def local_heads(heads):
-        chunks = [(h, first) for h in heads for first in range(0, tokens, QUERY_CHUNK)]
-
-        def scores_of(chunk):
-            h, first = chunk
-            t = h // 2
-            return dot(k_ref[:, t * LANES:(t + 1) * LANES], qt[h, :, first:first + QUERY_CHUNK])
-
-        ahead = scores_of(chunks[0])
-        for n, (h, first) in enumerate(chunks):
-            scores = ahead
-            if n + 1 < len(chunks):
-                ahead = scores_of(chunks[n + 1])
-            rows = slice(h * HEAD_SIZE, (h + 1) * HEAD_SIZE)
-            _, total, out = partial_softmax(scores, vt[rows], 1)
-            comb[rows, first:first + QUERY_CHUNK] = (out * (1.0 / total)).astype(jnp.bfloat16)
-
-    local_heads(range(0, 3))
-    for level in (1, 2) if chips[0] == 1 else (0, 1, 2):
-        forward(level)
-    local_heads(range(3, HEAD_COUNT))
-
-    parts = []
-    for t in range(PAIRS):
-        columns = slice(t * LANES, (t + 1) * LANES)
-        scores = dot(k_ref[:, columns], qbd[t], ((1,), (1,)))
-        parts.append([partial_softmax(scores, vt[columns], 1)])
+    after(HALF_FIRST, first_half)
+    if chips[0] > 1:
+        forward(0)
+    after(ALL_FIRST, second_half)
+    forward(1)
+    forward(2)
 
     def rows_of(buf, first):
         block = buf[:, :, :, first:first + LANES]
@@ -216,12 +236,15 @@
 
     to_mate(0).wait()
     for t in range(PAIRS):
-        parts[t].append(shared_level(near, t))
+        done = (tops[t], totals[t], sums[t])
+        tops[t], totals[t], sums[t] = join(done, shared_level(near, t))
 
     to_mate(1).wait()
     for t in range(PAIRS):
         top, total, out = shared_level(middle, t)
-        parts[t].append((jnp.where(lane_slot < 16, top, ABSENT), total, out))
+        done = (tops[t], totals[t], sums[t])
+        part = (jnp.where(lane_slot < 16, top, ABSENT), total, out)
+        tops[t], totals[t], sums[t] = join(done, part)
 
     to_mate(2).wait()
     scores = dot(rows_of(whole, 0), query, ((1,), (1,)))
@@ -232,8 +255,9 @@
     stores = []
     for t in range(PAIRS):
         columns = slice(t * LANES, (t + 1) * LANES)
-        parts[t].append((jnp.where((lane_slot >> 2) == t, top3, ABSENT), total3, out3))
-        merged = jnp.where(block_diagonal, join(parts[t]), 0.0).astype(jnp.bfloat16)
+        part = (jnp.where((lane_slot >> 2) == t, top3, ABSENT), total3, out3)
+        _, total, out = join((tops[t], totals[t], sums[t]), part)
+        merged = jnp.where(block_diagonal, out * (1.0 / total), 0.0).astype(jnp.bfloat16)
         placed = dot(merged, spread[t])
         head = 2 * t + (iota(placed.shape, 0) >> 6)
         chosen = (iota(placed.shape, 1) & (FIRST_DILATION - 1)) == head
@@ -270,6 +294,9 @@
             pltpu.VMEM((WIDTH, tokens), bf16),
             pltpu.VMEM((HEAD_COUNT, LANES, tokens), bf16),
             pltpu.VMEM((PAIRS, LANES, LANES), bf16),
+            pltpu.VMEM((PAIRS, 1, LANES), jnp.float32),
+            pltpu.VMEM((PAIRS, 1, LANES), jnp.float32),
+            pltpu.VMEM((PAIRS, LANES, LANES), jnp.float32),
             pltpu.VMEM((2, chips[0], slots, 2 * WIDTH), bf16),
             pltpu.VMEM((2, chips[1], slots // 4, 2 * WIDTH), bf16),
             pltpu.VMEM((2, chips[2], 16, 2 * LANES), bf16),

time: 16.8 us -> 15.4 us (0.917)
  Pallas kernels: 15.2 us -> 13.8 us
    pallas_call x1, Pallas kernels: 15.2 us -> 13.8 us  [on_device(): pl.pallas_call(functools.partial(kernel, chips), out_shape=jax.ShapeDtype...]
where the time goes in v3:
time: 15.4 us; the launch traced here: 15.3 us
  Pallas kernels  13.8 us (90%)
  matrix products  1.48 us (10%)
    pallas_call x1, Pallas kernels, on_device(): pl.pallas_call(functools.partial(kernel, chips), out_shape=jax.ShapeDtype...  13.8 us
    dot_general x1, matrix products, dot(): lax.dot_general(a, b, (dims, ((), ())), preferred_element_type=jnp.float32)  1.48 us

profile of v3, /device:TPU:0, one launch (start us, length us, event | category | flops | bytes accessed | tf_op | source)
XLA Modules:
  0.0 15.3 jit_solution(12771796933077630474)
XLA Ops:
  0.0 0.0 copy-start
  0.0 13.8 %shard_map.46 = bf16[384,512]{1,0:T(8,128)(2,1)S(1)} custom-call(bf16[512,384]{1,0:T(8,128)(2,1)} %q_hbm.1, bf16[512,384]{1,0:T(8,128)(2,1)} %k_hbm.1, bf16[512,384]{1,0:T(8,128)(2,1)} %v_hbm.1), custom_call_target="tpu_custom_call" | custom-call | flops 1000000000 | bytes 3000000 | tf_op jit(solution)/shard_map/pallas_call | solution.py:283
  13.8 0.0 copy-done
  13.8 1.5 %convolution_convert_fusion = bf16[512,768]{1,0:T(8,128)(2,1)} fusion(bf16[384,512]{1,0:T(8,128)(2,1)S(1)} %shard_map.46, bf16[384,768]{1,0:T(8,128)(2,1)S(1)} %copy-done), kind=kOutput, calls=%fused_computation | convolution fusion | flops 302383104 | bytes 1769472 | tf_op jit(solution)/shard_map/dot_general | solution.py:47
Async XLA Ops:
  0.0 13.8 %copy-start = (bf16[384,768]{1,0:T(8,128)(2,1)S(1)}, bf16[384,768]{1,0:T(8,128)(2,1)}, u32[]{:S(2)}) copy-start(bf16[384,768]{1,0:T(8,128)(2,1)} %param.7) | copy-start | bytes 1769476

commit v4 on v3

--- a/solution.py
+++ b/solution.py
@@ -62,9 +62,9 @@
 
 
 def kernel(
-    chips, q_hbm, k_hbm, v_hbm, out_hbm,
-    q_ref, k_ref, v_ref, comb, spread, vt, qt, qbd, tops, totals, sums, near, middle, whole,
-    in_sem, out_sem, send_sem, recv_sem, mate_send, mate_recv,
+    chips, q_hbm, k_hbm, v_hbm, comb,
+    q_ref, k_ref, v_ref, spread, vt, qt, qbd, tops, totals, sums, near, middle, whole,
+    in_sem, send_sem, recv_sem, mate_send, mate_recv,
 ):
     tokens = q_ref.shape[0]
     me = lax.axis_index("seq")
@@ -174,7 +174,7 @@
 
     pl.semaphore_wait(barrier, total_chips)
 
-    for level in (2, 1, 0):
+    for level in (1, 2, 0):
         own = bufs[level].at[core, places[level]]
 
         def send(d, level=level, own=own):
@@ -216,8 +216,6 @@
     if chips[0] > 1:
         forward(0)
     after(ALL_FIRST, second_half)
-    forward(1)
-    forward(2)
 
     def rows_of(buf, first):
         block = buf[:, :, :, first:first + LANES]
@@ -234,25 +232,27 @@
         query = jnp.where(slot_rows == t, qbd[t].astype(jnp.float32), query)
     query = query.astype(jnp.bfloat16)
 
-    to_mate(0).wait()
+    to_mate(0).wait_recv()
     for t in range(PAIRS):
         done = (tops[t], totals[t], sums[t])
         tops[t], totals[t], sums[t] = join(done, shared_level(near, t))
 
-    to_mate(1).wait()
+    forward(1)
+    forward(2)
+
+    to_mate(1).wait_recv()
     for t in range(PAIRS):
         top, total, out = shared_level(middle, t)
         done = (tops[t], totals[t], sums[t])
         part = (jnp.where(lane_slot < 16, top, ABSENT), total, out)
         tops[t], totals[t], sums[t] = join(done, part)
 
-    to_mate(2).wait()
+    to_mate(2).wait_recv()
     scores = dot(rows_of(whole, 0), query, ((1,), (1,)))
     row_pair = (iota(scores.shape, 0) & 15) >> 2
     scores = jnp.where(row_pair == (lane_slot >> 2), scores, ABSENT)
     top3, total3, out3 = partial_softmax(scores, rows_of(whole, LANES), 0)
 
-    stores = []
     for t in range(PAIRS):
         columns = slice(t * LANES, (t + 1) * LANES)
         part = (jnp.where((lane_slot >> 2) == t, top3, ABSENT), total3, out3)
@@ -264,14 +264,11 @@
         comb[columns] = jnp.where(
             chosen, placed, comb[columns].astype(jnp.float32)
         ).astype(jnp.bfloat16)
-        stores.append(pltpu.make_async_copy(comb.at[columns], out_hbm.at[columns], out_sem.at[t]))
-        stores[-1].start()
 
     for level in range(3):
+        to_mate(level).wait_send()
         if chips[level] > 1:
             others(level, send_sem).wait()
-    for store in stores:
-        store.wait()
 
 
 def on_device(queries, keys, values, out_weight):
@@ -284,12 +281,11 @@
         functools.partial(kernel, chips),
         out_shape=jax.ShapeDtypeStruct((WIDTH, tokens), bf16),
         in_specs=[pl.BlockSpec(memory_space=pl.ANY)] * 3,
-        out_specs=pl.BlockSpec(memory_space=pl.ANY),
+        out_specs=pl.BlockSpec(memory_space=pltpu.VMEM),
         scratch_shapes=[
             pltpu.VMEM(queries.shape, bf16),
             pltpu.VMEM(keys.shape, bf16),
             pltpu.VMEM(values.shape, bf16),
-            pltpu.VMEM((WIDTH, tokens), bf16),
             pltpu.VMEM((PAIRS, LANES, tokens), bf16),
             pltpu.VMEM((WIDTH, tokens), bf16),
             pltpu.VMEM((HEAD_COUNT, LANES, tokens), bf16),
@@ -301,7 +297,6 @@
             pltpu.VMEM((2, chips[1], slots // 4, 2 * WIDTH), bf16),
             pltpu.VMEM((2, chips[2], 16, 2 * LANES), bf16),
             pltpu.SemaphoreType.DMA((3,)),
-            pltpu.SemaphoreType.DMA((PAIRS,)),
             pltpu.SemaphoreType.DMA((3,)),
             pltpu.SemaphoreType.DMA((3,)),
             pltpu.SemaphoreType.DMA((3,)),

time: 15.4 us -> 14.2 us (0.922)
  the two profiles are of different devices: /device:TPU:0 before, /device:TPU:1 now
where the time goes in v4:
time: 14.2 us; the launch traced here: 14 us
  Pallas kernels  12.5 us (88%)
  matrix products  1.48 us (10%)
    pallas_call x1, Pallas kernels, on_device(): pl.pallas_call(functools.partial(kernel, chips), out_shape=jax.ShapeDtype...  12.5 us
    dot_general x1, matrix products, dot(): lax.dot_general(a, b, (dims, ((), ())), preferred_element_type=jnp.float32)  1.48 us

profile of v4, /device:TPU:1, one launch (start us, length us, event | category | flops | bytes accessed | tf_op | source)
XLA Modules:
  0.0 14.0 jit_solution(3382056303586303245)
XLA Ops:
  0.0 0.0 copy-start
  0.0 12.5 %shard_map.46 = bf16[384,512]{1,0:T(8,128)(2,1)S(1)} custom-call(bf16[512,384]{1,0:T(8,128)(2,1)} %q_hbm.1, bf16[512,384]{1,0:T(8,128)(2,1)} %k_hbm.1, bf16[512,384]{1,0:T(8,128)(2,1)} %v_hbm.1), custom_call_target="tpu_custom_call" | custom-call | flops 1000000000 | bytes 3000000 | tf_op jit(solution)/shard_map/pallas_call | solution.py:280
  12.5 0.0 copy-done
  12.6 1.5 %convolution_convert_fusion = bf16[512,768]{1,0:T(8,128)(2,1)} fusion(bf16[384,512]{1,0:T(8,128)(2,1)S(1)} %shard_map.46, bf16[384,768]{1,0:T(8,128)(2,1)S(1)} %copy-done), kind=kOutput, calls=%fused_computation | convolution fusion | flops 302383104 | bytes 1769472 | tf_op jit(solution)/shard_map/dot_general | solution.py:47
Async XLA Ops:
  0.0 12.5 %copy-start = (bf16[384,768]{1,0:T(8,128)(2,1)S(1)}, bf16[384,768]{1,0:T(8,128)(2,1)}, u32[]{:S(2)}) copy-start(bf16[384,768]{1,0:T(8,128)(2,1)} %param.7) | copy-start | bytes 1769476

commit v5 on v4

--- a/solution.py
+++ b/solution.py
@@ -247,6 +247,13 @@
         part = (jnp.where(lane_slot < 16, top, ABSENT), total, out)
         tops[t], totals[t], sums[t] = join(done, part)
 
+    for t in range(PAIRS):
+        columns = slice(t * LANES, (t + 1) * LANES)
+        head = 2 * t + (iota((LANES, tokens), 0) >> 6)
+        chosen = (iota((LANES, tokens), 1) & (FIRST_DILATION - 1)) == head
+        alone = comb[columns].astype(jnp.float32)
+        comb[columns] = jnp.where(chosen, 0.0, alone).astype(jnp.bfloat16)
+
     to_mate(2).wait_recv()
     scores = dot(rows_of(whole, 0), query, ((1,), (1,)))
     row_pair = (iota(scores.shape, 0) & 15) >> 2
@@ -259,11 +266,7 @@
         _, total, out = join((tops[t], totals[t], sums[t]), part)
         merged = jnp.where(block_diagonal, out * (1.0 / total), 0.0).astype(jnp.bfloat16)
         placed = dot(merged, spread[t])
-        head = 2 * t + (iota(placed.shape, 0) >> 6)
-        chosen = (iota(placed.shape, 1) & (FIRST_DILATION - 1)) == head
-        comb[columns] = jnp.where(
-            chosen, placed, comb[columns].astype(jnp.float32)
-        ).astype(jnp.bfloat16)
+        comb[columns] = (comb[columns].astype(jnp.float32) + placed).astype(jnp.bfloat16)
 
     for level in range(3):
         to_mate(level).wait_send()

time: 14.2 us -> 14.2 us (level)
  no operation moved by 1% of the time
where the time goes in v5:
time: 14.2 us; the launch traced here: 14.1 us
  Pallas kernels  12.6 us (89%)
  matrix products  1.48 us (10%)
    pallas_call x1, Pallas kernels, on_device(): pl.pallas_call(functools.partial(kernel, chips), out_shape=jax.ShapeDtype...  12.6 us
    dot_general x1, matrix products, dot(): lax.dot_general(a, b, (dims, ((), ())), preferred_element_type=jnp.float32)  1.48 us

profile of v5, /device:TPU:1, one launch (start us, length us, event | category | flops | bytes accessed | tf_op | source)
XLA Modules:
  0.0 14.1 jit_solution(4026502199335760124)
XLA Ops:
  0.0 0.0 copy-start
  0.0 12.6 %shard_map.46 = bf16[384,512]{1,0:T(8,128)(2,1)S(1)} custom-call(bf16[512,384]{1,0:T(8,128)(2,1)} %q_hbm.1, bf16[512,384]{1,0:T(8,128)(2,1)} %k_hbm.1, bf16[512,384]{1,0:T(8,128)(2,1)} %v_hbm.1), custom_call_target="tpu_custom_call" | custom-call | flops 1000000000 | bytes 3000000 | tf_op jit(solution)/shard_map/pallas_call | solution.py:283
  12.6 0.0 copy-done
  12.6 1.5 %convolution_convert_fusion = bf16[512,768]{1,0:T(8,128)(2,1)} fusion(bf16[384,512]{1,0:T(8,128)(2,1)S(1)} %shard_map.46, bf16[384,768]{1,0:T(8,128)(2,1)S(1)} %copy-done), kind=kOutput, calls=%fused_computation | convolution fusion | flops 302383104 | bytes 1769472 | tf_op jit(solution)/shard_map/dot_general | solution.py:47
Async XLA Ops:
  0.0 12.6 %copy-start = (bf16[384,768]{1,0:T(8,128)(2,1)S(1)}, bf16[384,768]{1,0:T(8,128)(2,1)}, u32[]{:S(2)}) copy-start(bf16[384,768]{1,0:T(8,128)(2,1)} %param.7) | copy-start | bytes 1769476
